TPU v7x, 32 devices: a whole 2x2x4 slice. The times are simulated.
32 devices in a mesh: row: 8 (over z, y), col: 4 (over x, core).
Axes of the slice: x: 2, y: 2, z: 4, core: 2. Of those that a mesh axis runs over, the one named last changes fastest.
Arguments:
- blocks: bfloat16 [512, 12, 128, 128], P('row'), may hold values from -0.15625 to 0.15625
- col_index: int32 [512, 12], P('row'), may hold values from -8 to 519, as said below
- live_slots: int32 [512], P('row'), may hold values from 3 to 12, as said below
- vectors: bfloat16 [256, 65536], P('col', 'row'), may hold values from -6 to 6
- center: float32 [1], replicated, may hold values from -0.4 to 0.4
- halfwidth: float32 [1], replicated, may hold values from 0.8 to 1.6
Outputs:
- ortho_basis: float32 [256, 65536], P('col', 'row')
- triangle: float32 [256, 256], replicated
Inputs may be any that keep to these rules, and one draw needn't show every extreme that they name: col_index[i, k] - i lies in -8 .. 8 and is different for every k of a row; slot 0 is i, slot 1 is i + 8, slot 2 is i - 8. `live_slots`: slots 0, 1 and 2 are live in every row; the counts of one index of row lie within one of a level shared by that index (block rows 0 and 1 excepted), so whole devices are busy or light.
All inputs are finite; a program needn't handle non-finite values.
Results may differ from a plain program's by a relative error of at most 0.0042.
Values may be sent and summed in bfloat16 or wider, within the bound.
A program may use at most 128 MiB of HBM per device.

v0:
```python
import jax
import jax.numpy as jnp
from jax import lax
from jax.sharding import PartitionSpec as P

W = 8


def padded(array, sides, width):
    for axis, dim in sides:
        devices, length = (lax.axis_size(axis), array.shape[dim])
        up = [(i, (i + 1) % devices) for i in range(devices - 1)]
        down = [(j, i) for i, j in up]
        last = lax.slice_in_dim(array, length - width, length, axis=dim)
        initial = lax.slice_in_dim(array, 0, width, axis=dim)
        before = lax.ppermute(last, axis, up)
        after = lax.ppermute(initial, axis, down)
        array = jnp.concatenate([before, array, after], axis=dim)
    return array


def apply_blocks(blocks, local_index, live_slots, field):
    width = field.shape[0]
    rows_block = blocks.shape[2]
    block_rows = blocks.shape[0]
    slots = blocks.shape[1]
    extended = padded(field, (("row", 1),), W * rows_block)
    extended = extended.reshape(width, block_rows + 2 * W, rows_block)
    slot_live = jnp.arange(slots, dtype=jnp.int32)[None, :] < live_slots[:, None]
    picked = jnp.take(extended, local_index.reshape(-1), axis=1).reshape(
        width, block_rows, slots, rows_block
    )
    picked = jnp.where(slot_live[None, :, :, None], picked, jnp.zeros((), jnp.bfloat16))
    product = jnp.einsum("rkab,vrkb->vra", blocks, picked, preferred_element_type=jnp.float32)
    return product.reshape(width, block_rows * rows_block)


def invert_lower(factor):
    total_vectors = factor.shape[0]
    identity = jnp.eye(total_vectors, dtype=jnp.float32)
    return lax.linalg.triangular_solve(factor, identity, left_side=True, lower=True)


def on_device(blocks, col_index, live_slots, vectors, center, halfwidth):
    block_rows = blocks.shape[0]
    row_count = vectors.shape[1]
    local_cols = vectors.shape[0]
    order_all = row_count * lax.axis_size("row")
    start_block = lax.axis_index("row") * block_rows
    local_index = col_index - start_block + W
    shift_value = center[0]
    scale_value = halfwidth[0]
    plain = vectors.astype(jnp.float32)
    first_step = (
        (apply_blocks(blocks, local_index, live_slots, vectors) - shift_value * plain) / scale_value
    ).astype(jnp.bfloat16)
    second = apply_blocks(blocks, local_index, live_slots, first_step)
    filtered = (
        2.0 * (second - shift_value * first_step.astype(jnp.float32)) / scale_value - plain
    ).astype(jnp.bfloat16)
    contract = (((1,), (1,)), ((), ()))
    all_columns = lax.all_gather(filtered, "col", axis=0, tiled=True)
    partial_gram = lax.dot_general(
        all_columns, all_columns, contract, preferred_element_type=jnp.float32
    )
    gram_matrix = lax.psum(partial_gram, "row") / order_all
    factor = jnp.linalg.cholesky(gram_matrix)
    inverse = invert_lower(factor)
    own_rows = lax.dynamic_slice_in_dim(inverse, lax.axis_index("col") * local_cols, local_cols, 0)
    ortho_basis = jnp.dot(
        own_rows, all_columns.astype(jnp.float32), precision=lax.Precision.HIGHEST
    )
    return (ortho_basis, factor.T)


def solution(mesh):
    in_specs = (P("row", None, None, None), P("row", None), P("row"), P("col", "row"), P(), P())
    out_specs = (P("col", "row"), P())
    return jax.shard_map(
        on_device, mesh=mesh, in_specs=in_specs, out_specs=out_specs, check_vma=False
    )
```

profile of v0, /device:TPU:0, one launch (start us, length us, event | category | flops | bytes accessed | tf_op | source)
XLA Modules:
  0.0 313.0 jit_solution(4013367620410499459)
XLA Ops:
  8.2 4.9 %collective-permute-start = (bf16[64,1024]{1,0:T(8,128)(2,1)S(1)}, bf16[64,1024]{1,0:T(8,128)(2,1)S(1)}, u32[]{:S(2)}, u32[]{:S(2)}) collective-permute-start(bf16[64,1024]{1,0:T(8,128)(2,1)S(1)} %get-tuple-element.29), channel_id=1, source_target_pairs={{0,4},{4,8},{8,12},{12,16},{16,20},{20,24},{24,28},{1,5},{5,9},{9,... | collective-permute-start | bytes 393224 | tf_op jit(solution)/shard_map/ppermute | solution.py:16
  17.4 2.6 collective-permute-done.1
  19.9 1.6 copy_bitcast_fusion.1
  21.5 18.2 %gather_fusion = bf16[768,64,128]{2,1,0:T(8,128)(2,1)} fusion(bf16[64,80,128]{2,0,1:T(8,128)(2,1)S(1)} %copy_bitcast_fusion.1, s32[1024]{0:T(1024)S(1)} %pad_clamp_fusion), kind=kCustom, calls=%fused_computation.clone | custom fusion | bytes 25168896 | tf_op jit(solution)/shard_map/jit(_take)/gather | solution.py:30
  39.7 11.3 %broadcast_select_fusion = bf16[768,64,128]{2,1,0:T(8,128)(2,1)} fusion(bf16[768,64,128]{2,1,0:T(8,128)(2,1)} %gather_fusion, pred[768]{0:T(1024)(128)(4,1)S(1)} %compare_and_fusion), kind=kLoop, calls=%fused_computation.8 | loop fusion | flops 6291456 | bytes 25166592 | tf_op jit(solution)/shard_map/jit(_take)/select_n | solution.py:30
  51.0 15.7 %fusion.14 = f32[64,8,8,128]{3,2,1,0:T(8,128)S(1)} fusion(bf16[64,12,128,128]{3,2,1,0:T(8,128)(2,1)} %param.8, bf16[64,64,12,128]{3,0,2,1:T(8,128)(2,1)} %bitcast.83, pred[64,12]{1,0:T(8,128)(4,1)S(1)} %iota_compare_fusion.4), kind=kOutput, calls=%fused_computation.23 | convolution fusion | flops 1616904192 | bytes 39846656 | tf_op jit(solution)/shard_map/rkab,vrkb->vra/dot_general | solution.py:34
  67.1 4.3 %collective-permute-start.2 = (bf16[64,1024]{1,0:T(8,128)(2,1)S(1)}, bf16[64,1024]{1,0:T(8,128)(2,1)S(1)}, u32[]{:S(2)}, u32[]{:S(2)}) collective-permute-start(bf16[64,1024]{1,0:T(8,128)(2,1)S(1)} %get-tuple-element.27), channel_id=1, source_target_pairs={{0,4},{4,8},{8,12},{12,16},{16,20},{20,24},{24,28},{1,5},{5,9},{9,... | collective-permute-start | bytes 393224 | tf_op jit(solution)/shard_map/ppermute | solution.py:16
  71.4 1.5 collective-permute-start.3
  73.9 4.4 %collective-permute-done.3 = bf16[64,1024]{1,0:T(8,128)(2,1)S(1)} collective-permute-done((bf16[64,1024]{1,0:T(8,128)(2,1)S(1)}, bf16[64,1024]{1,0:T(8,128)(2,1)S(1)}, u32[]{:S(2)}, u32[]{:S(2)}) %collective-permute-start.3) | collective-permute-done | bytes 131104 | tf_op jit(solution)/shard_map/ppermute | solution.py:17
  78.7 18.2 %gather_fusion.1 = bf16[768,64,128]{2,1,0:T(8,128)(2,1)} fusion(bf16[64,80,128]{2,0,1:T(8,128)(2,1)S(1)} %copy_bitcast_fusion, s32[1024]{0:T(1024)S(1)} %pad_clamp_fusion), kind=kCustom, calls=%fused_computation.1.clone | custom fusion | bytes 25168896 | tf_op jit(solution)/shard_map/jit(_take)/gather | solution.py:30
  96.9 11.3 %broadcast_select_fusion.1 = bf16[768,64,128]{2,1,0:T(8,128)(2,1)} fusion(bf16[768,64,128]{2,1,0:T(8,128)(2,1)} %gather_fusion.1, pred[768]{0:T(1024)(128)(4,1)S(1)} %compare_and_fusion), kind=kLoop, calls=%fused_computation.9 | loop fusion | flops 6291456 | bytes 25166592 | tf_op jit(solution)/shard_map/jit(_take)/select_n | solution.py:30
  108.2 15.6 %fusion.17 = f32[64,8,8,128]{3,2,1,0:T(8,128)S(1)} fusion(bf16[64,12,128,128]{3,2,1,0:T(8,128)(2,1)} %param.8, bf16[64,64,12,128]{3,0,2,1:T(8,128)(2,1)} %bitcast.82, pred[64,12]{1,0:T(8,128)(4,1)S(1)} %iota_compare_fusion.4), kind=kOutput, calls=%fused_computation.24 | convolution fusion | flops 1616904192 | bytes 39846656 | tf_op jit(solution)/shard_map/rkab,vrkb->vra/dot_general | solution.py:34
  123.8 1.5 fusion.11
  125.6 35.1 %all-gather.2.cloned.1.call-done = bf16[256,8192]{1,0:T(8,128)(2,1)} async-done(((bf16[64,8192]{1,0:T(8,128)(2,1)}), bf16[256,8192]{1,0:T(8,128)(2,1)}) %all-gather.2.cloned.1.call-update) | async-done | bytes 4194320 | tf_op jit(solution)/shard_map/all_gather | solution.py:62
  160.7 5.4 %fusion.40 = f32[256,256]{0,1:T(8,128)} fusion(bf16[256,8192]{1,0:T(8,128)(2,1)} %all-gather.2.cloned.1.call-done), kind=kOutput, calls=%fused_computation.74 | convolution fusion | flops 1073741824 | bytes 4456448 | tf_op jit(solution)/shard_map/dot_general | solution.py:63
  166.2 70.6 %all-reduce.3.cloned.1.call-done = f32[256,256]{0,1:T(8,128)} async-done(((f32[256,256]{0,1:T(8,128)}), f32[256,256]{0,1:T(8,128)}) %all-reduce.3.cloned.1.call-update) | async-done | bytes 262160 | tf_op jit(solution)/shard_map/psum | solution.py:66
  239.0 11.7 %cholesky.50 = f32[128,128]{1,0:T(8,128)S(1)} custom-call(f32[128,128]{1,0:T(8,128)S(1)} %cholesky.118), custom_call_target="Cholesky" | custom-call | tf_op jit(solution)/shard_map/jit(cholesky)/cholesky | solution.py:67
  250.7 9.8 %custom-call.14 = f32[1,128,128]{1,2,0:T(8,128)S(1)} custom-call(f32[1,128,128]{2,1,0:T(8,128)S(1)} %get-tuple-element.36), custom_call_target="InvertDiagBlocksLowerTriangular" | custom-call | tf_op jit(solution)/shard_map/jit(cholesky)/cholesky | solution.py:67
  261.0 11.7 %cholesky.105 = f32[128,128]{1,0:T(8,128)S(1)} custom-call(f32[128,128]{1,0:T(8,128)S(1)} %convolution_subtract_fusion.1), custom_call_target="Cholesky" | custom-call | tf_op jit(solution)/shard_map/jit(cholesky)/cholesky | solution.py:67
  274.8 4.1 %while.1 = (s32[]{:T(128)}, f32[256,256]{1,0:T(8,128)S(1)}, s32[2,2]{1,0:T(2,128)S(1)}, f32[2,128,128]{2,1,0:T(8,128)S(1)}, s32[]{:T(128)}) while((s32[]{:T(128)}, f32[256,256]{1,0:T(8,128)S(1)}, s32[2,2]{1,0:T(2,128)S(1)}, f32[2,128,128]{2,1,0:T(8,128)S(1)}, s32[]{:T(128)}) %tuple.34), condition=%wide.while_cond, body=%wide.while_body.sunk | while | flops 2 | bytes 131181 | solution.py:41
  275.7 1.3 bitcast_dynamic-update-slice_fusion.2
  277.6 1.3 bitcast_dynamic-update-slice_fusion.2
  279.0 19.7 %custom-call.15 = f32[2,128,128]{1,2,0:T(8,128)S(1)} custom-call(f32[2,128,128]{2,1,0:T(8,128)S(1)} %get-tuple-element.10), custom_call_target="InvertDiagBlocksLowerTriangular" | custom-call | tf_op jit(solution)/shard_map/triangular_solve | solution.py:41
  300.4 5.8 %fusion.26 = f32[64,8192]{1,0:T(8,128)} fusion(bf16[256,8192]{1,0:T(8,128)(2,1)} %all-gather.2.cloned.1.call-done, s32[]{:T(128)S(6)} %select_n.24, f32[128,256]{1,0:T(8,128)S(1)} %fusion.23, f32[128,256]{1,0:T(8,128)S(1)} %fusion.29), kind=kOutput, calls=%fused_computation.44 | convolution fusion | flops 1610629120 | bytes 6553604 | tf_op jit(solution)/shard_map/dot_general | solution.py:70
  (43 shorter events, 12.3 us)
Async XLA Ops:
  7.2 153.6 %all-gather.2.cloned.1.call-start = ((), (), s32[]{:S(2)}) async-start(), calls=%async_computation | async-start | bytes 5242880 | tf_op jit(solution)/shard_map/all_gather | solution.py:62
  8.2 9.2 %collective-permute-start = (bf16[64,1024]{1,0:T(8,128)(2,1)S(1)}, bf16[64,1024]{1,0:T(8,128)(2,1)S(1)}, u32[]{:S(2)}, u32[]{:S(2)}) collective-permute-start(bf16[64,1024]{1,0:T(8,128)(2,1)S(1)} %get-tuple-element.29), channel_id=1, source_target_pairs={{0,4},{4,8},{8,12},{12,16},{16,20},{20,24},{24,28},{1,5},{5,9},{9,... | collective-permute-start | bytes 393224 | tf_op jit(solution)/shard_map/ppermute | solution.py:16
  13.1 6.9 %collective-permute-start.1 = (bf16[64,1024]{1,0:T(8,128)(2,1)S(1)}, bf16[64,1024]{1,0:T(8,128)(2,1)S(1)}, u32[]{:S(2)}, u32[]{:S(2)}) collective-permute-start(bf16[64,1024]{1,0:T(8,128)(2,1)S(1)} %get-tuple-element.30), channel_id=1, source_target_pairs={{4,0},{8,4},{12,8},{16,12},{20,16},{24,20},{28,24},{5,1},{9,5},{13... | collective-permute-start | bytes 393224 | tf_op jit(solution)/shard_map/ppermute | solution.py:17
  51.0 15.7 %copy-start = (bf16[64,8192]{1,0:T(8,128)(2,1)S(1)}, bf16[64,8192]{1,0:T(8,128)(2,1)}, u32[]{:S(2)}) copy-start(bf16[64,8192]{1,0:T(8,128)(2,1)} %param.11) | copy-start | bytes 3145732
  67.1 6.8 %collective-permute-start.2 = (bf16[64,1024]{1,0:T(8,128)(2,1)S(1)}, bf16[64,1024]{1,0:T(8,128)(2,1)S(1)}, u32[]{:S(2)}, u32[]{:S(2)}) collective-permute-start(bf16[64,1024]{1,0:T(8,128)(2,1)S(1)} %get-tuple-element.27), channel_id=1, source_target_pairs={{0,4},{4,8},{8,12},{12,16},{16,20},{20,24},{24,28},{1,5},{5,9},{9,... | collective-permute-start | bytes 393224 | tf_op jit(solution)/shard_map/ppermute | solution.py:16
  71.4 6.9 %collective-permute-start.3 = (bf16[64,1024]{1,0:T(8,128)(2,1)S(1)}, bf16[64,1024]{1,0:T(8,128)(2,1)S(1)}, u32[]{:S(2)}, u32[]{:S(2)}) collective-permute-start(bf16[64,1024]{1,0:T(8,128)(2,1)S(1)} %get-tuple-element.28), channel_id=1, source_target_pairs={{4,0},{8,4},{12,8},{16,12},{20,16},{24,20},{28,24},{5,1},{9,5},{13... | collective-permute-start | bytes 393224 | tf_op jit(solution)/shard_map/ppermute | solution.py:17
  125.3 111.6 %all-reduce.3.cloned.1.call-start = ((), (), s32[]{:S(2)}) async-start(), calls=%async_computation.1 | async-start | bytes 524288 | tf_op jit(solution)/shard_map/psum | solution.py:66
Sparse Core Ops, SparseCore 0:
  125.4 35.2 all-gather.1
  166.3 70.5 all-reduce.2
where the time goes:
time: 314 us; the launch traced here: 313 us
  waiting for transfers between devices  114 us (36%)
  other arithmetic  83.6 us (27%)
  matrix products  43.8 us (14%)
  local copies, waits for them, and re-layouts  42.5 us (14%)
  between operations  16.9 us (5%)
  starting transfers between devices  12.3 us (4%)
    psum x1, waiting for transfers between devices, on_device(): gram_matrix = lax.psum(partial_gram, 'row') / order_all  70.6 us
    gather x2, local copies, waits for them, and re-layouts, apply_blocks(): jnp.take(extended, local_index.reshape(-1), axis=1)  36.4 us
    all_gather x1, waiting for transfers between devices, on_device(): all_columns = lax.all_gather(filtered, 'col', axis=0, tiled=True)  35.1 us
    another operation x6, other arithmetic, on_device(): factor = jnp.linalg.cholesky(gram_matrix)  34 us
    dot_general x2, matrix products, apply_blocks(): jnp.einsum('rkab,vrkb->vra', blocks, picked, preferred_element_type=jnp.f...  31.3 us
    select_n x3, other arithmetic, apply_blocks(): jnp.take(extended, local_index.reshape(-1), axis=1)  22.6 us
    another operation x2, other arithmetic, invert_lower(): lax.linalg.triangular_solve(factor, identity, left_side=True, lower=True)  19.7 us
    ppermute x2, starting transfers between devices, padded(): before = lax.ppermute(last, axis, up)  9.21 us
  transfers between devices with their start and end apart: 6, of which 5 were waited for; matrix products, arithmetic and copies ran while one was open for 1% of the time, Pallas kernels for 0%

commit v1 on v0

v1 whole, which is shorter than its diff:
```python
import functools

import jax
import jax.numpy as jnp
from jax import lax
from jax.experimental import pallas as pl
from jax.experimental.pallas import tpu as pltpu
from jax.sharding import PartitionSpec as P

W = 8
VMEM_BYTES = 56 * 1024 * 1024
NT = (((1,), (1,)), ((), ()))
TN = (((0,), (0,)), ((), ()))
NN = (((1,), (0,)), ((), ()))
HIGHEST = lax.Precision.HIGHEST


def halo(array, width):
    devices, length = lax.axis_size("row"), array.shape[1]
    up = [(i, (i + 1) % devices) for i in range(devices - 1)]
    down = [(j, i) for i, j in up]
    before = lax.ppermute(array[:, length - width :], "row", up)
    after = lax.ppermute(array[:, :width], "row", down)
    return before, after


def product_kernel(
    second, slots, per_step, index, live, shift, scale, blocks, before, field, after, *rest
):
    plain, out, extended = rest if second else (None, *rest)
    side = blocks.shape[2]
    step = pl.program_id(0)

    @pl.when(step == 0)
    def _():
        for i in range(W):
            extended[i] = before[:, i * side : (i + 1) * side]
            extended[extended.shape[0] - W + i] = after[:, i * side : (i + 1) * side]
        for i in range(extended.shape[0] - 2 * W):
            extended[W + i] = field[:, i * side : (i + 1) * side]

    inverse_scale = 1.0 / scale[0]
    for r in range(per_step):
        row = step * per_step + r
        count = live[row]
        picked = []
        for k in range(slots):
            value = extended[index[row * slots + k]]
            if k >= 3:
                value = jnp.where(k < count, value, jnp.zeros_like(value))
            picked.append(value)
        picked = jnp.concatenate(picked, axis=1)
        stored = jnp.concatenate([blocks[r, k] for k in range(slots)], axis=1)
        product = lax.dot_general(picked, stored, NT, preferred_element_type=jnp.float32)
        own = extended[W + row].astype(jnp.float32)
        value = (product - shift[0] * own) * inverse_scale
        if second:
            value = 2.0 * value - plain[:, r * side : (r + 1) * side].astype(jnp.float32)
        out[:, r * side : (r + 1) * side] = value.astype(out.dtype)


def product(blocks, index, live, shift, scale, field, plain=None):
    block_rows, slots, side, _ = blocks.shape
    width, length = field.shape
    before, after = halo(field, W * side)
    per_step = 4
    smem = pl.BlockSpec(memory_space=pltpu.SMEM)
    whole = pl.BlockSpec(memory_space=pltpu.VMEM)
    tile = pl.BlockSpec((width, per_step * side), lambda i: (0, i))
    second = plain is not None
    return pl.pallas_call(
        functools.partial(product_kernel, second, slots, per_step),
        grid=(block_rows // per_step,),
        out_shape=jax.ShapeDtypeStruct((width, length), jnp.bfloat16),
        in_specs=[smem] * 4
        + [pl.BlockSpec((per_step, slots, side, side), lambda i: (i, 0, 0, 0))]
        + [whole] * 3
        + ([tile] if second else []),
        out_specs=tile,
        scratch_shapes=[pltpu.VMEM((block_rows + 2 * W, width, side), jnp.bfloat16)],
        compiler_params=pltpu.CompilerParams(vmem_limit_bytes=VMEM_BYTES),
        cost_estimate=pl.CostEstimate(
            flops=2 * blocks.size * width, bytes_accessed=2 * blocks.size, transcendentals=0
        ),
    )(index, live, shift, scale, blocks, before, field, after, *([plain] if second else []))


def dot32(a, b, dims):
    return lax.dot_general(a, b, dims, precision=HIGHEST, preferred_element_type=jnp.float32)


def factor_block(matrix):
    n = matrix.shape[0]
    groups = [matrix[8 * g : 8 * g + 8] for g in range(n // 8)]
    lane = lax.broadcasted_iota(jnp.int32, (8, n), 1)
    sub = lax.broadcasted_iota(jnp.int32, (8, n), 0)
    upper = []
    for p in range(n // 8):
        panel = groups[p]
        saved = jnp.zeros_like(panel)
        for j in range(8):
            c = 8 * p + j
            column = jnp.broadcast_to(panel[:, c : c + 1], (8, n))
            pivot = jnp.broadcast_to(panel[j : j + 1, c : c + 1], (8, n))
            line = jnp.broadcast_to(panel[j : j + 1, :], (8, n))
            root = lax.rsqrt(pivot)
            line = line * root
            saved = jnp.where((sub == j) & (lane >= c), line, saved)
            line = jnp.where(lane == c, root, line)
            below = jnp.where(lane == c, 0.0, panel) - (column * root) * line
            panel = jnp.where(sub > j, below, jnp.where(sub == j, line, panel))
        upper.append(saved)
        inside = (lane >= 8 * p) & (lane < 8 * p + 8)
        panel = jnp.where(inside & (lane - 8 * p > sub), 0.0, panel)
        groups[p] = panel
        if p + 1 < n // 8:
            change = dot32(saved, panel, TN)
            for g in range(p + 1, n // 8):
                kept = jnp.where(inside, 0.0, groups[g])
                groups[g] = kept - change[8 * g : 8 * g + 8]
    row = lax.broadcasted_iota(jnp.int32, (n, n), 0)
    col = lax.broadcasted_iota(jnp.int32, (n, n), 1)
    inverse = jnp.where(row >= col, jnp.concatenate(groups, axis=0), 0.0)
    return jnp.concatenate(upper, axis=0), inverse


def finish_kernel(order, own_group, gram, field, basis, triangle, inverse):
    @pl.when(pl.program_id(0) == 0)
    def _():
        size = gram.shape[0]
        h = size // 2
        triangle[...] = jnp.zeros_like(triangle)
        inverse[...] = jnp.zeros_like(inverse)
        scaled = 1.0 / order
        u11, z11 = factor_block(gram[:h, :h] * scaled)
        u12 = dot32(z11, gram[:h, h:] * scaled, NN)
        u22, z22 = factor_block(gram[h:, h:] * scaled - dot32(u12, u12, TN))
        z21 = -dot32(z22, dot32(u12, z11, TN), NN)
        triangle[:h, :h] = u11
        triangle[:h, h:] = u12
        triangle[h:, h:] = u22
        inverse[:h, :h] = z11
        inverse[h:, :h] = z21
        inverse[h:, h:] = z22

    width = basis.shape[0]
    start = pl.multiple_of(own_group[0] * width, width)
    rows = inverse[pl.ds(start, width), :]
    high = rows.astype(jnp.bfloat16)
    left = rows - high.astype(jnp.float32)
    low = left.astype(jnp.bfloat16)
    rest = (left - low.astype(jnp.float32)).astype(jnp.bfloat16)
    both = jnp.concatenate([high, low, rest], axis=0)
    wide = jnp.dot(both, field[...], preferred_element_type=jnp.float32)
    basis[...] = wide[:width] + (wide[width : 2 * width] + wide[2 * width :])


def finish(gram, field, order, width):
    size, length = field.shape
    tile = min(length, 2048)
    group = lax.axis_index("col").astype(jnp.int32).reshape(1)
    whole = pl.BlockSpec((size, size), lambda i: (0, 0))
    return pl.pallas_call(
        functools.partial(finish_kernel, order),
        grid=(length // tile,),
        out_shape=(
            jax.ShapeDtypeStruct((width, length), jnp.float32),
            jax.ShapeDtypeStruct((size, size), jnp.float32),
        ),
        in_specs=[
            pl.BlockSpec(memory_space=pltpu.SMEM),
            whole,
            pl.BlockSpec((size, tile), lambda i: (0, i)),
        ],
        out_specs=(pl.BlockSpec((width, tile), lambda i: (0, i)), whole),
        scratch_shapes=[pltpu.VMEM((size, size), jnp.float32)],
        compiler_params=pltpu.CompilerParams(vmem_limit_bytes=VMEM_BYTES),
    )(group, gram, field)


def on_device(blocks, col_index, live_slots, vectors, center, halfwidth):
    block_rows = blocks.shape[0]
    order_all = vectors.shape[1] * lax.axis_size("row")
    index = (col_index - lax.axis_index("row") * block_rows + W).reshape(-1)
    first_step = product(blocks, index, live_slots, center, halfwidth, vectors)
    filtered = product(blocks, index, live_slots, center, halfwidth, first_step, vectors)
    all_columns = lax.all_gather(filtered, "col", axis=0, tiled=True)
    partial_gram = lax.dot_general(
        all_columns, all_columns, NT, preferred_element_type=jnp.float32
    )
    gram = lax.psum(partial_gram, "row")
    basis, triangle = finish(gram, all_columns, order_all, vectors.shape[0])
    return (basis, triangle)


def solution(mesh):
    in_specs = (P("row", None, None, None), P("row", None), P("row"), P("col", "row"), P(), P())
    out_specs = (P("col", "row"), P())
    return jax.shard_map(
        on_device, mesh=mesh, in_specs=in_specs, out_specs=out_specs, check_vma=False
    )
```

time: 314 us -> 235 us (0.75)
  other arithmetic: 83.6 us -> 0.7 us
  Pallas kernels: 0 us -> 82.2 us
  local copies, waits for them, and re-layouts: 42.5 us -> 4.08 us
  matrix products: 43.8 us -> 5.45 us
    pallas_call x0 -> x3, Pallas kernels: none -> 82.2 us  [the longest x1 43 us: finish(): pl.pallas_call(functools.partial(finish_kernel, order), grid=(length // t...]
    another operation x8 -> x0, other arithmetic: 53.7 us -> none  [the longest x6 34 us: on_device(): factor = jnp.linalg.cholesky(gram_matrix)]
    dot_general x4 -> x1, matrix products: 42.5 us -> 5.45 us  [on_device(): lax.dot_general(all_columns, all_columns, NT, preferred_element_type=jnp....]
    gather x2 -> x0, local copies, waits for them, and re-layouts: 36.4 us -> none  [apply_blocks(): jnp.take(extended, local_index.reshape(-1), axis=1)]
    select_n x3 -> x0, other arithmetic: 22.6 us -> none  [apply_blocks(): jnp.take(extended, local_index.reshape(-1), axis=1)]
    another operation x9 -> x0, local copies, waits for them, and re-layouts: 3.97 us -> none
where the time goes in v1:
time: 235 us; the launch traced here: 234 us
  waiting for transfers between devices  113 us (48%)
  Pallas kernels  82.2 us (35%)
  between operations  15.4 us (7%)
  starting transfers between devices  13.2 us (6%)
  matrix products  5.45 us (2%)
  local copies, waits for them, and re-layouts  4.08 us (2%)
    psum x1, waiting for transfers between devices, on_device(): gram = lax.psum(partial_gram, 'row')  70.8 us
    pallas_call x1, Pallas kernels, finish(): pl.pallas_call(functools.partial(finish_kernel, order), grid=(length // t...  43 us
    pallas_call x2, Pallas kernels, product(): pl.pallas_call(functools.partial(product_kernel, second, slots, per_step)...  39.2 us
    all_gather x1, waiting for transfers between devices, on_device(): all_columns = lax.all_gather(filtered, 'col', axis=0, tiled=True)  36.1 us
    ppermute x2, starting transfers between devices, halo(): before = lax.ppermute(array[:, length - width:], 'row', up)  10.5 us
    dot_general x1, matrix products, on_device(): lax.dot_general(all_columns, all_columns, NT, preferred_element_type=jnp....  5.45 us
  transfers between devices with their start and end apart: 6, of which 5 were waited for; matrix products, arithmetic and copies ran while one was open for 1% of the time, Pallas kernels for 0%

profile of v1, /device:TPU:0, one launch (start us, length us, event | category | flops | bytes accessed | tf_op | source)
XLA Modules:
  0.0 234.3 jit_solution(1763176659266429232)
XLA Ops:
  7.2 0.0 all-gather.2.cloned.1.call-start
  7.2 1.0 fusion.1
  8.2 1.3 collective-permute-start.1
  9.5 5.5 %collective-permute-start = (bf16[64,1024]{1,0:T(8,128)(2,1)S(1)}, bf16[64,1024]{1,0:T(8,128)(2,1)S(1)}, u32[]{:S(2)}, u32[]{:S(2)}) collective-permute-start(bf16[64,1024]{1,0:T(8,128)(2,1)S(1)} %get-tuple-element.5), channel_id=1, source_target_pairs={{0,4},{4,8},{8,12},{12,16},{16,20},{20,24},{24,28},{1,5},{5,9},{9,... | collective-permute-start | bytes 393224 | tf_op jit(solution)/shard_map/ppermute | solution.py:22
  16.3 0.7 subtract_add_fusion
  17.0 0.1 copy.8
  17.1 0.7 reshape.11.index
  17.8 1.7 collective-permute-done.before
  19.5 0.7 copy-done.1
  20.2 19.6 %shard_map.77.field = bf16[64,8192]{1,0:T(8,128)(2,1)} custom-call(s32[768]{0:T(1024)} %reshape.11.index, s32[64]{0:T(128)} %live.3, f32[1]{0:T(128)S(6)} %copy.10.shift, f32[1]{0:T(128)S(6)} %copy.11.scale, bf16[64,12,128,128]{3,2,1,0:T(8,128)(2,1)} %blocks.3, bf16[64,1024]{1,0:T(8,128)(2,1)} %copy-done.1, bf16[64,8192]{1,0:T(8,128)(2,1)} %rest_0_.1, ...), custom_call_target="tpu_custom_call" | custom-call | flops 1610612736 | bytes 25165824 | tf_op jit(solution)/shard_map/pallas_call | solution.py:71
  39.7 1.0 fusion
  40.7 1.3 collective-permute-start.3
  42.0 5.0 %collective-permute-start.2 = (bf16[64,1024]{1,0:T(8,128)(2,1)S(1)}, bf16[64,1024]{1,0:T(8,128)(2,1)S(1)}, u32[]{:S(2)}, u32[]{:S(2)}) collective-permute-start(bf16[64,1024]{1,0:T(8,128)(2,1)S(1)} %get-tuple-element.3), channel_id=1, source_target_pairs={{0,4},{4,8},{8,12},{12,16},{16,20},{20,24},{24,28},{1,5},{5,9},{9,... | collective-permute-start | bytes 393224 | tf_op jit(solution)/shard_map/ppermute | solution.py:22
  47.1 1.7 collective-permute-done.3.after
  48.8 3.0 %collective-permute-done.2.before = bf16[64,1024]{1,0:T(8,128)(2,1)S(1)} collective-permute-done((bf16[64,1024]{1,0:T(8,128)(2,1)S(1)}, bf16[64,1024]{1,0:T(8,128)(2,1)S(1)}, u32[]{:S(2)}, u32[]{:S(2)}) %collective-permute-start.2) | collective-permute-done | bytes 131104 | tf_op jit(solution)/shard_map/ppermute | solution.py:22
  51.8 0.7 copy-done.3
  52.4 19.6 %shard_map.78 = bf16[64,8192]{1,0:T(8,128)(2,1)} custom-call(s32[768]{0:T(1024)} %reshape.11.index, s32[64]{0:T(128)} %live.3, f32[1]{0:T(128)S(6)} %copy.10.shift, f32[1]{0:T(128)S(6)} %copy.11.scale, bf16[64,12,128,128]{3,2,1,0:T(8,128)(2,1)} %blocks.3, bf16[64,1024]{1,0:T(8,128)(2,1)} %copy-done.3, bf16[64,8192]{1,0:T(8,128)(2,1)} %shard_map.77.field, ...), custom_call_target="tpu_custom_call" | custom-call | flops 1610612736 | bytes 25165824 | tf_op jit(solution)/shard_map/pallas_call | solution.py:71
  72.1 0.0 all-gather.2.cloned.1.call-update
  72.1 0.0 all-reduce.2.cloned.1.call-start
  72.1 36.1 %all-gather.2.cloned.1.call-done.field = bf16[256,8192]{1,0:T(8,128)(2,1)} async-done(((bf16[64,8192]{1,0:T(8,128)(2,1)}), bf16[256,8192]{1,0:T(8,128)(2,1)}) %all-gather.2.cloned.1.call-update) | async-done | bytes 4194320 | tf_op jit(solution)/shard_map/all_gather | solution.py:187
  108.2 5.4 %fusion.2 = f32[256,256]{1,0:T(8,128)} fusion(bf16[256,8192]{1,0:T(8,128)(2,1)} %all-gather.2.cloned.1.call-done.field), kind=kOutput, calls=%fused_computation.3 | convolution fusion | flops 1073741824 | bytes 4456448 | tf_op jit(solution)/shard_map/dot_general | solution.py:188
  113.6 0.0 all-reduce.2.cloned.1.call-update
  113.7 70.8 %all-reduce.2.cloned.1.call-done.gram = f32[256,256]{1,0:T(8,128)} async-done(((f32[256,256]{1,0:T(8,128)}), f32[256,256]{1,0:T(8,128)}) %all-reduce.2.cloned.1.call-update) | async-done | bytes 262160 | tf_op jit(solution)/shard_map/psum | solution.py:191
  184.4 43.0 %shard_map.79 = (f32[64,8192]{1,0:T(8,128)}, f32[256,256]{1,0:T(8,128)}) custom-call(s32[1]{0:T(128)} %bitcast.own_group, f32[256,256]{1,0:T(8,128)} %all-reduce.2.cloned.1.call-done.gram, bf16[256,8192]{1,0:T(8,128)(2,1)} %all-gather.2.cloned.1.call-done.field), custom_call_target="tpu_custom_call" | custom-call | tf_op jit(solution)/shard_map/pallas_call | solution.py:163
  (7 shorter events, 0.0 us)
Async XLA Ops:
  7.2 101.0 %all-gather.2.cloned.1.call-start = ((), (), s32[]{:S(2)}) async-start(), calls=%async_computation | async-start | bytes 5242880 | tf_op jit(solution)/shard_map/all_gather | solution.py:187
  8.2 9.6 %collective-permute-start.1 = (bf16[64,1024]{1,0:T(8,128)(2,1)S(1)}, bf16[64,1024]{1,0:T(8,128)(2,1)S(1)}, u32[]{:S(2)}, u32[]{:S(2)}) collective-permute-start(bf16[64,1024]{1,0:T(8,128)(2,1)S(1)} %get-tuple-element.4), channel_id=1, source_target_pairs={{4,0},{8,4},{12,8},{16,12},{20,16},{24,20},{28,24},{5,1},{9,5},{13... | collective-permute-start | bytes 393224 | tf_op jit(solution)/shard_map/ppermute | solution.py:23
  9.5 10.0 %collective-permute-start = (bf16[64,1024]{1,0:T(8,128)(2,1)S(1)}, bf16[64,1024]{1,0:T(8,128)(2,1)S(1)}, u32[]{:S(2)}, u32[]{:S(2)}) collective-permute-start(bf16[64,1024]{1,0:T(8,128)(2,1)S(1)} %get-tuple-element.5), channel_id=1, source_target_pairs={{0,4},{4,8},{8,12},{12,16},{16,20},{20,24},{24,28},{1,5},{5,9},{9,... | collective-permute-start | bytes 393224 | tf_op jit(solution)/shard_map/ppermute | solution.py:22
  17.8 1.7 copy-start
  19.5 0.7 copy-start.1
  40.7 8.1 %collective-permute-start.3 = (bf16[64,1024]{1,0:T(8,128)(2,1)S(1)}, bf16[64,1024]{1,0:T(8,128)(2,1)S(1)}, u32[]{:S(2)}, u32[]{:S(2)}) collective-permute-start(bf16[64,1024]{1,0:T(8,128)(2,1)S(1)} %get-tuple-element.2), channel_id=1, source_target_pairs={{4,0},{8,4},{12,8},{16,12},{20,16},{24,20},{28,24},{5,1},{9,5},{13... | collective-permute-start | bytes 393224 | tf_op jit(solution)/shard_map/ppermute | solution.py:23
  42.0 9.7 %collective-permute-start.2 = (bf16[64,1024]{1,0:T(8,128)(2,1)S(1)}, bf16[64,1024]{1,0:T(8,128)(2,1)S(1)}, u32[]{:S(2)}, u32[]{:S(2)}) collective-permute-start(bf16[64,1024]{1,0:T(8,128)(2,1)S(1)} %get-tuple-element.3), channel_id=1, source_target_pairs={{0,4},{4,8},{8,12},{12,16},{16,20},{20,24},{24,28},{1,5},{5,9},{9,... | collective-permute-start | bytes 393224 | tf_op jit(solution)/shard_map/ppermute | solution.py:22
  48.8 3.0 %copy-start.2 = (bf16[64,1024]{1,0:T(8,128)(2,1)}, bf16[64,1024]{1,0:T(8,128)(2,1)S(1)}, u32[]{:S(2)}) copy-start(bf16[64,1024]{1,0:T(8,128)(2,1)S(1)} %collective-permute-done.3.after) | copy-start | bytes 393220
  51.8 0.7 copy-start.3
  72.1 112.4 %all-reduce.2.cloned.1.call-start = ((), (), s32[]{:S(2)}) async-start(), calls=%async_computation.1 | async-start | bytes 524288 | tf_op jit(solution)/shard_map/psum | solution.py:191
Sparse Core Ops, SparseCore 0:
  72.2 35.9 all-gather.1
  113.8 70.5 all-reduce.1

commit v2 on v1

--- a/solution.py
+++ b/solution.py
@@ -178,17 +178,176 @@
     )(group, gram, field)
 
 
+def gather_gram_kernel(own, everyone, gram, parts, inbox, gathered, chunk_send, chunk_recv, sems):
+    rows, cols = lax.axis_size("row"), lax.axis_size("col")
+    devices = rows * cols
+    row, col = lax.axis_index("row"), lax.axis_index("col")
+    me = row * cols + col
+    width, length = own.shape
+    chunk = length // cols
+
+    def target(offset):
+        flat = lax.rem(me + offset, devices)
+        return {"row": lax.div(flat, cols), "col": lax.rem(flat, cols)}
+
+    def flip(value, mask):
+        for bit in bits:
+            if mask & bit:
+                value = value + bit * (1 - 2 * lax.rem(lax.div(value, bit), 2))
+        return value
+
+    bits = [1 << b for b in reversed(range(cols.bit_length() - 1))]
+    barrier = pltpu.get_barrier_semaphore()
+
+    def greet(offset, carry):
+        pl.semaphore_signal(
+            barrier, inc=1, device_id=target(offset), device_id_type=pl.DeviceIdType.MESH
+        )
+        return carry
+
+    lax.fori_loop(1, devices, greet, 0)
+    everyone[col] = own[...]
+    pl.semaphore_wait(barrier, devices - 1)
+
+    def piece(bit, mask, order):
+        peer = flip(col, bit)
+        place = pl.ds(pl.multiple_of(flip(peer, order) * chunk, 128), chunk)
+        slot = slots[(bit, mask)] * cols + order
+        view = everyone.at[flip(col, mask), :, place]
+        return pltpu.make_async_remote_copy(
+            src_ref=view,
+            dst_ref=view,
+            send_sem=chunk_send.at[slot],
+            recv_sem=chunk_recv.at[slot],
+            device_id={"row": row, "col": peer},
+            device_id_type=pl.DeviceIdType.MESH,
+        )
+
+    slots, held, plan = {}, [0], []
+    for bit in bits:
+        for mask in held:
+            slots[(bit, mask)] = len(slots)
+            plan.append((bit, mask))
+        held = held + [m ^ bit for m in held]
+    waited = set()
+
+    def arrived(bit, mask, order):
+        if (bit, mask, order) not in waited:
+            waited.add((bit, mask, order))
+            piece(bit, mask, order).wait_recv()
+
+    for order in range(cols):
+        for bit in bits:
+            piece(bit, 0, order).start()
+    for order in range(cols):
+        for bit, mask in plan:
+            if mask:
+                came = mask & -mask
+                arrived(came, mask ^ came, bit ^ order)
+                piece(bit, mask, order).start()
+        if order == 0 or cols == 1:
+            for bit, mask in plan:
+                arrived(bit, mask, 0)
+            share = everyone[:, :, pl.ds(pl.multiple_of(col * chunk, 128), chunk)]
+            share = share.reshape(cols * width, chunk)
+            partial = lax.dot_general(share, share, NT, preferred_element_type=jnp.float32)
+            held_rows = parts.shape[1]
+            for i in range(devices):
+                parts[i] = partial[i * held_rows : (i + 1) * held_rows]
+
+            def scatter(offset, carry):
+                flat = lax.rem(me + offset, devices)
+                pltpu.make_async_remote_copy(
+                    src_ref=parts.at[flat],
+                    dst_ref=inbox.at[offset - 1],
+                    send_sem=sems.at[0],
+                    recv_sem=sems.at[1],
+                    device_id=target(offset),
+                    device_id_type=pl.DeviceIdType.MESH,
+                ).start()
+                return carry
+
+            lax.fori_loop(1, devices, scatter, 0)
+
+    def settle(send, recv):
+        return pltpu.make_async_remote_copy(
+            src_ref=inbox,
+            dst_ref=inbox,
+            send_sem=sems.at[send],
+            recv_sem=sems.at[recv],
+            device_id=target(1),
+            device_id_type=pl.DeviceIdType.MESH,
+        )
+
+    settle(0, 1).wait_recv()
+    total = parts[me]
+    for i in range(devices - 1):
+        total = total + inbox[i]
+    gathered[me] = total
+
+    def spread(offset, carry):
+        pltpu.make_async_remote_copy(
+            src_ref=gathered.at[me],
+            dst_ref=gathered.at[me],
+            send_sem=sems.at[2],
+            recv_sem=sems.at[3],
+            device_id=target(offset),
+            device_id_type=pl.DeviceIdType.MESH,
+        ).start()
+        return carry
+
+    lax.fori_loop(1, devices, spread, 0)
+    settle(2, 3).wait_recv()
+    for i in range(devices):
+        gram[i * parts.shape[1] : (i + 1) * parts.shape[1]] = gathered[i]
+    for order in range(cols):
+        for bit, mask in plan:
+            arrived(bit, mask, order)
+    for order in range(cols):
+        for bit, mask in plan:
+            piece(bit, mask, order).wait_send()
+    settle(0, 1).wait_send()
+    settle(2, 3).wait_send()
+
+
+def gather_gram(own):
+    cols = lax.axis_size("col")
+    devices = cols * lax.axis_size("row")
+    width, length = own.shape
+    size = width * cols
+    share = size // devices
+    whole = pl.BlockSpec(memory_space=pltpu.VMEM)
+    pieces = (cols - 1) * cols
+    everyone, gram = pl.pallas_call(
+        gather_gram_kernel,
+        out_shape=(
+            jax.ShapeDtypeStruct((cols, width, length), own.dtype),
+            jax.ShapeDtypeStruct((size, size), jnp.float32),
+        ),
+        in_specs=[whole],
+        out_specs=(whole, whole),
+        scratch_shapes=[
+            pltpu.VMEM((devices, share, size), jnp.float32),
+            pltpu.VMEM((devices - 1, share, size), jnp.float32),
+            pltpu.VMEM((devices, share, size), jnp.float32),
+            pltpu.SemaphoreType.DMA((pieces,)),
+            pltpu.SemaphoreType.DMA((pieces,)),
+            pltpu.SemaphoreType.DMA((4,)),
+        ],
+        compiler_params=pltpu.CompilerParams(
+            collective_id=0, has_side_effects=True, vmem_limit_bytes=VMEM_BYTES
+        ),
+    )(own)
+    return everyone.reshape(size, length), gram
+
+
 def on_device(blocks, col_index, live_slots, vectors, center, halfwidth):
     block_rows = blocks.shape[0]
     order_all = vectors.shape[1] * lax.axis_size("row")
     index = (col_index - lax.axis_index("row") * block_rows + W).reshape(-1)
     first_step = product(blocks, index, live_slots, center, halfwidth, vectors)
     filtered = product(blocks, index, live_slots, center, halfwidth, first_step, vectors)
-    all_columns = lax.all_gather(filtered, "col", axis=0, tiled=True)
-    partial_gram = lax.dot_general(
-        all_columns, all_columns, NT, preferred_element_type=jnp.float32
-    )
-    gram = lax.psum(partial_gram, "row")
+    all_columns, gram = gather_gram(filtered)
     basis, triangle = finish(gram, all_columns, order_all, vectors.shape[0])
     return (basis, triangle)
 

time: 235 us -> 152 us (0.65)
  waiting for transfers between devices: 113 us -> 6.4 us
  Pallas kernels: 82.2 us -> 125 us
  between operations: 15.4 us -> 1.98 us
  matrix products: 5.45 us -> 0 us
    psum x1 -> x0, waiting for transfers between devices: 70.8 us -> none  [on_device(): gram = lax.psum(partial_gram, 'row')]
    pallas_call x0 -> x1, Pallas kernels: none -> 42.7 us  [gather_gram(): pl.pallas_call(gather_gram_kernel, out_shape=(jax.ShapeDtypeStruct((cols,...]
    all_gather x1 -> x0, waiting for transfers between devices: 36.1 us -> none  [on_device(): all_columns = lax.all_gather(filtered, 'col', axis=0, tiled=True)]
    dot_general x1 -> x0, matrix products: 5.45 us -> none  [on_device(): lax.dot_general(all_columns, all_columns, NT, preferred_element_type=jnp....]
  transfers between devices with their start and end apart: 6 -> 4, of which waited for: 5 -> 3; matrix products, arithmetic and copies ran while one was open for 1% -> 1% of each run, Pallas kernels for 0% -> 0%
where the time goes in v2:
time: 152 us; the launch traced here: 151 us
  Pallas kernels  125 us (82%)
  starting transfers between devices  13.1 us (9%)
  waiting for transfers between devices  6.4 us (4%)
  local copies, waits for them, and re-layouts  4.08 us (3%)
  between operations  1.98 us (1%)
    pallas_call x1, Pallas kernels, finish(): pl.pallas_call(functools.partial(finish_kernel, order), grid=(length // t...  43 us
    pallas_call x1, Pallas kernels, gather_gram(): pl.pallas_call(gather_gram_kernel, out_shape=(jax.ShapeDtypeStruct((cols,...  42.7 us
    pallas_call x2, Pallas kernels, product(): pl.pallas_call(functools.partial(product_kernel, second, slots, per_step)...  39.2 us
    ppermute x2, starting transfers between devices, halo(): before = lax.ppermute(array[:, length - width:], 'row', up)  10.5 us
    ppermute x2, waiting for transfers between devices, halo(): before = lax.ppermute(array[:, length - width:], 'row', up)  4.67 us
  transfers between devices with their start and end apart: 4, of which 3 were waited for; matrix products, arithmetic and copies ran while one was open for 1% of the time, Pallas kernels for 0%

profile of v2, /device:TPU:0, one launch (start us, length us, event | category | flops | bytes accessed | tf_op | source)
XLA Modules:
  0.0 151.1 jit_solution(6950307971661967310)
XLA Ops:
  0.6 1.0 fusion.1
  1.6 1.3 collective-permute-start.1
  2.9 5.5 %collective-permute-start = (bf16[64,1024]{1,0:T(8,128)(2,1)S(1)}, bf16[64,1024]{1,0:T(8,128)(2,1)S(1)}, u32[]{:S(2)}, u32[]{:S(2)}) collective-permute-start(bf16[64,1024]{1,0:T(8,128)(2,1)S(1)} %get-tuple-element.9), channel_id=1, source_target_pairs={{0,4},{4,8},{8,12},{12,16},{16,20},{20,24},{24,28},{1,5},{5,9},{9,... | collective-permute-start | bytes 393224 | tf_op jit(solution)/shard_map/ppermute | solution.py:22
  9.7 0.7 subtract_add_fusion
  10.4 0.1 copy.8
  10.5 0.7 reshape.14.index
  11.2 0.0 collective-permute-done.1.after
  11.2 0.0 copy-start
  11.2 1.7 %collective-permute-done.before = bf16[64,1024]{1,0:T(8,128)(2,1)S(1)} collective-permute-done((bf16[64,1024]{1,0:T(8,128)(2,1)S(1)}, bf16[64,1024]{1,0:T(8,128)(2,1)S(1)}, u32[]{:S(2)}, u32[]{:S(2)}) %collective-permute-start) | collective-permute-done | bytes 131104 | tf_op jit(solution)/shard_map/ppermute | solution.py:22
  12.9 0.0 copy-done
  12.9 0.0 copy-start.1
  12.9 0.7 copy-done.1
  13.6 19.6 %shard_map.77.field = bf16[64,8192]{1,0:T(8,128)(2,1)} custom-call(s32[768]{0:T(1024)} %reshape.14.index, s32[64]{0:T(128)} %live.3, f32[1]{0:T(128)S(6)} %copy.9.shift, f32[1]{0:T(128)S(6)} %copy.10.scale, bf16[64,12,128,128]{3,2,1,0:T(8,128)(2,1)} %blocks.3, bf16[64,1024]{1,0:T(8,128)(2,1)} %copy-done.1, bf16[64,8192]{1,0:T(8,128)(2,1)} %rest_0_.1, ...), custom_call_target="tpu_custom_call" | custom-call | flops 1610612736 | bytes 25165824 | tf_op jit(solution)/shard_map/pallas_call | solution.py:71
  33.2 1.0 fusion
  34.1 1.3 collective-permute-start.3
  35.4 5.0 %collective-permute-start.2 = (bf16[64,1024]{1,0:T(8,128)(2,1)S(1)}, bf16[64,1024]{1,0:T(8,128)(2,1)S(1)}, u32[]{:S(2)}, u32[]{:S(2)}) collective-permute-start(bf16[64,1024]{1,0:T(8,128)(2,1)S(1)} %get-tuple-element.7), channel_id=1, source_target_pairs={{0,4},{4,8},{8,12},{12,16},{16,20},{20,24},{24,28},{1,5},{5,9},{9,... | collective-permute-start | bytes 393224 | tf_op jit(solution)/shard_map/ppermute | solution.py:22
  40.5 1.7 %collective-permute-done.3.after = bf16[64,1024]{1,0:T(8,128)(2,1)S(1)} collective-permute-done((bf16[64,1024]{1,0:T(8,128)(2,1)S(1)}, bf16[64,1024]{1,0:T(8,128)(2,1)S(1)}, u32[]{:S(2)}, u32[]{:S(2)}) %collective-permute-start.3) | collective-permute-done | bytes 131104 | tf_op jit(solution)/shard_map/ppermute | solution.py:23
  42.2 0.0 copy-start.2
  42.2 3.0 %collective-permute-done.2.before = bf16[64,1024]{1,0:T(8,128)(2,1)S(1)} collective-permute-done((bf16[64,1024]{1,0:T(8,128)(2,1)S(1)}, bf16[64,1024]{1,0:T(8,128)(2,1)S(1)}, u32[]{:S(2)}, u32[]{:S(2)}) %collective-permute-start.2) | collective-permute-done | bytes 131104 | tf_op jit(solution)/shard_map/ppermute | solution.py:22
  45.2 0.0 copy-done.2
  45.2 0.7 copy-done.3
  45.8 19.6 %shard_map.78.own = bf16[64,8192]{1,0:T(8,128)(2,1)} custom-call(s32[768]{0:T(1024)} %reshape.14.index, s32[64]{0:T(128)} %live.3, f32[1]{0:T(128)S(6)} %copy.9.shift, f32[1]{0:T(128)S(6)} %copy.10.scale, bf16[64,12,128,128]{3,2,1,0:T(8,128)(2,1)} %blocks.3, bf16[64,1024]{1,0:T(8,128)(2,1)} %copy-done.3, bf16[64,8192]{1,0:T(8,128)(2,1)} %shard_map.77.field, ...), custom_call_target="tpu_custom_call" | custom-call | flops 1610612736 | bytes 25165824 | tf_op jit(solution)/shard_map/pallas_call | solution.py:71
  65.5 42.7 %shard_map.79 = (bf16[4,64,8192]{2,1,0:T(8,128)(2,1)}, f32[256,256]{1,0:T(8,128)}) custom-call(bf16[64,8192]{1,0:T(8,128)(2,1)} %shard_map.78.own), custom_call_target="tpu_custom_call" | custom-call | tf_op jit(solution)/shard_map/pallas_call | solution.py:321
  108.1 43.0 %shard_map.80 = (f32[64,8192]{1,0:T(8,128)}, f32[256,256]{1,0:T(8,128)}) custom-call(s32[1]{0:T(128)} %bitcast.own_group, f32[256,256]{1,0:T(8,128)} %get-tuple-element.4.gram, bf16[256,8192]{1,0:T(8,128)(2,1)} %bitcast.2), custom_call_target="tpu_custom_call" | custom-call | tf_op jit(solution)/shard_map/pallas_call | solution.py:163
  (1 shorter events, 0.0 us)
Async XLA Ops:
  1.6 9.6 %collective-permute-start.1 = (bf16[64,1024]{1,0:T(8,128)(2,1)S(1)}, bf16[64,1024]{1,0:T(8,128)(2,1)S(1)}, u32[]{:S(2)}, u32[]{:S(2)}) collective-permute-start(bf16[64,1024]{1,0:T(8,128)(2,1)S(1)} %get-tuple-element.8), channel_id=1, source_target_pairs={{4,0},{8,4},{12,8},{16,12},{20,16},{24,20},{28,24},{5,1},{9,5},{13... | collective-permute-start | bytes 393224 | tf_op jit(solution)/shard_map/ppermute | solution.py:23
  2.9 10.0 %collective-permute-start = (bf16[64,1024]{1,0:T(8,128)(2,1)S(1)}, bf16[64,1024]{1,0:T(8,128)(2,1)S(1)}, u32[]{:S(2)}, u32[]{:S(2)}) collective-permute-start(bf16[64,1024]{1,0:T(8,128)(2,1)S(1)} %get-tuple-element.9), channel_id=1, source_target_pairs={{0,4},{4,8},{8,12},{12,16},{16,20},{20,24},{24,28},{1,5},{5,9},{9,... | collective-permute-start | bytes 393224 | tf_op jit(solution)/shard_map/ppermute | solution.py:22
  11.2 1.7 %copy-start = (bf16[64,1024]{1,0:T(8,128)(2,1)}, bf16[64,1024]{1,0:T(8,128)(2,1)S(1)}, u32[]{:S(2)}) copy-start(bf16[64,1024]{1,0:T(8,128)(2,1)S(1)} %collective-permute-done.1.after) | copy-start | bytes 393220
  12.9 0.7 copy-start.1
  34.1 8.1 %collective-permute-start.3 = (bf16[64,1024]{1,0:T(8,128)(2,1)S(1)}, bf16[64,1024]{1,0:T(8,128)(2,1)S(1)}, u32[]{:S(2)}, u32[]{:S(2)}) collective-permute-start(bf16[64,1024]{1,0:T(8,128)(2,1)S(1)} %get-tuple-element.6), channel_id=1, source_target_pairs={{4,0},{8,4},{12,8},{16,12},{20,16},{24,20},{28,24},{5,1},{9,5},{13... | collective-permute-start | bytes 393224 | tf_op jit(solution)/shard_map/ppermute | solution.py:23
  35.4 9.7 %collective-permute-start.2 = (bf16[64,1024]{1,0:T(8,128)(2,1)S(1)}, bf16[64,1024]{1,0:T(8,128)(2,1)S(1)}, u32[]{:S(2)}, u32[]{:S(2)}) collective-permute-start(bf16[64,1024]{1,0:T(8,128)(2,1)S(1)} %get-tuple-element.7), channel_id=1, source_target_pairs={{0,4},{4,8},{8,12},{12,16},{16,20},{20,24},{24,28},{1,5},{5,9},{9,... | collective-permute-start | bytes 393224 | tf_op jit(solution)/shard_map/ppermute | solution.py:22
  42.2 3.0 %copy-start.2 = (bf16[64,1024]{1,0:T(8,128)(2,1)}, bf16[64,1024]{1,0:T(8,128)(2,1)S(1)}, u32[]{:S(2)}) copy-start(bf16[64,1024]{1,0:T(8,128)(2,1)S(1)} %collective-permute-done.3.after) | copy-start | bytes 393220
  45.2 0.7 copy-start.3

commit v3 on v2

--- a/solution.py
+++ b/solution.py
@@ -51,7 +51,7 @@
             picked.append(value)
         picked = jnp.concatenate(picked, axis=1)
         stored = jnp.concatenate([blocks[r, k] for k in range(slots)], axis=1)
-        product = lax.dot_general(picked, stored, NT, preferred_element_type=jnp.float32)
+        product = lax.dot_general(stored, picked, NT, preferred_element_type=jnp.float32).T
         own = extended[W + row].astype(jnp.float32)
         value = (product - shift[0] * own) * inverse_scale
         if second:
@@ -63,7 +63,7 @@
     block_rows, slots, side, _ = blocks.shape
     width, length = field.shape
     before, after = halo(field, W * side)
-    per_step = 4
+    per_step = 8
     smem = pl.BlockSpec(memory_space=pltpu.SMEM)
     whole = pl.BlockSpec(memory_space=pltpu.VMEM)
     tile = pl.BlockSpec((width, per_step * side), lambda i: (0, i))
@@ -95,29 +95,48 @@
     lane = lax.broadcasted_iota(jnp.int32, (8, n), 1)
     sub = lax.broadcasted_iota(jnp.int32, (8, n), 0)
     upper = []
+
+    def spread_row(value, j):
+        return jnp.broadcast_to(value[j : j + 1, :], (8, n))
+
+    def spread_columns(value, p):
+        return [
+            jnp.broadcast_to(value[:, 8 * p + m : 8 * p + m + 1], (8, n)) for m in range(8)
+        ]
+
     for p in range(n // 8):
         panel = groups[p]
+        columns = spread_columns(panel, p)
         saved = jnp.zeros_like(panel)
+        roots, factors = [], []
         for j in range(8):
             c = 8 * p + j
-            column = jnp.broadcast_to(panel[:, c : c + 1], (8, n))
-            pivot = jnp.broadcast_to(panel[j : j + 1, c : c + 1], (8, n))
-            line = jnp.broadcast_to(panel[j : j + 1, :], (8, n))
-            root = lax.rsqrt(pivot)
-            line = line * root
+            root = lax.rsqrt(spread_row(columns[j], j))
+            scaled = columns[j] * root
+            across = [spread_row(scaled, m) for m in range(j + 1, 8)]
+            for m in range(j + 1, 8):
+                columns[m] = columns[m] - scaled * across[m - j - 1]
+            roots.append(root)
+            factors.append(across)
+            line = spread_row(panel, j) * root
             saved = jnp.where((sub == j) & (lane >= c), line, saved)
             line = jnp.where(lane == c, root, line)
-            below = jnp.where(lane == c, 0.0, panel) - (column * root) * line
+            below = jnp.where(lane == c, 0.0, panel) - scaled * line
             panel = jnp.where(sub > j, below, jnp.where(sub == j, line, panel))
         upper.append(saved)
         inside = (lane >= 8 * p) & (lane < 8 * p + 8)
         panel = jnp.where(inside & (lane - 8 * p > sub), 0.0, panel)
         groups[p] = panel
-        if p + 1 < n // 8:
-            change = dot32(saved, panel, TN)
-            for g in range(p + 1, n // 8):
-                kept = jnp.where(inside, 0.0, groups[g])
-                groups[g] = kept - change[8 * g : 8 * g + 8]
+        lines = [spread_row(panel, j) for j in range(8)]
+        for g in range(p + 1, n // 8):
+            columns = spread_columns(groups[g], p)
+            rest = jnp.where(inside, 0.0, groups[g])
+            for j in range(8):
+                scaled = columns[j] * roots[j]
+                for m in range(j + 1, 8):
+                    columns[m] = columns[m] - scaled * factors[j][m - j - 1]
+                rest = rest - scaled * lines[j]
+            groups[g] = rest
     row = lax.broadcasted_iota(jnp.int32, (n, n), 0)
     col = lax.broadcasted_iota(jnp.int32, (n, n), 1)
     inverse = jnp.where(row >= col, jnp.concatenate(groups, axis=0), 0.0)
@@ -236,38 +255,46 @@
             waited.add((bit, mask, order))
             piece(bit, mask, order).wait_recv()
 
-    for order in range(cols):
-        for bit in bits:
-            piece(bit, 0, order).start()
-    for order in range(cols):
-        for bit, mask in plan:
-            if mask:
-                came = mask & -mask
-                arrived(came, mask ^ came, bit ^ order)
-                piece(bit, mask, order).start()
-        if order == 0 or cols == 1:
+    def launch(orders):
+        for order in orders:
             for bit, mask in plan:
-                arrived(bit, mask, 0)
-            share = everyone[:, :, pl.ds(pl.multiple_of(col * chunk, 128), chunk)]
-            share = share.reshape(cols * width, chunk)
-            partial = lax.dot_general(share, share, NT, preferred_element_type=jnp.float32)
-            held_rows = parts.shape[1]
-            for i in range(devices):
-                parts[i] = partial[i * held_rows : (i + 1) * held_rows]
-
-            def scatter(offset, carry):
-                flat = lax.rem(me + offset, devices)
-                pltpu.make_async_remote_copy(
-                    src_ref=parts.at[flat],
-                    dst_ref=inbox.at[offset - 1],
-                    send_sem=sems.at[0],
-                    recv_sem=sems.at[1],
-                    device_id=target(offset),
-                    device_id_type=pl.DeviceIdType.MESH,
-                ).start()
-                return carry
-
-            lax.fori_loop(1, devices, scatter, 0)
+                if mask == 0:
+                    piece(bit, mask, order).start()
+
+    def forward(orders):
+        for order in orders:
+            for bit, mask in plan:
+                if mask:
+                    came = mask & -mask
+                    arrived(came, mask ^ came, bit ^ order)
+                    piece(bit, mask, order).start()
+
+    early = (cols + 1) // 2
+    launch(range(early))
+    forward(range(early))
+    for bit, mask in plan:
+        arrived(bit, mask, 0)
+    share = everyone[:, :, pl.ds(pl.multiple_of(col * chunk, 128), chunk)]
+    share = share.reshape(cols * width, chunk)
+    partial = lax.dot_general(share, share, NT, preferred_element_type=jnp.float32)
+    held_rows = parts.shape[1]
+    for i in range(devices):
+        parts[i] = partial[i * held_rows : (i + 1) * held_rows]
+
+    def scatter(offset, carry):
+        flat = lax.rem(me + offset, devices)
+        pltpu.make_async_remote_copy(
+            src_ref=parts.at[flat],
+            dst_ref=inbox.at[offset - 1],
+            send_sem=sems.at[0],
+            recv_sem=sems.at[1],
+            device_id=target(offset),
+            device_id_type=pl.DeviceIdType.MESH,
+        ).start()
+        return carry
+
+    lax.fori_loop(1, devices, scatter, 0)
+    launch(range(early, cols))
 
     def settle(send, recv):
         return pltpu.make_async_remote_copy(
@@ -297,6 +324,7 @@
         return carry
 
     lax.fori_loop(1, devices, spread, 0)
+    forward(range(early, cols))
     settle(2, 3).wait_recv()
     for i in range(devices):
         gram[i * parts.shape[1] : (i + 1) * parts.shape[1]] = gathered[i]

time: 152 us -> 114 us (0.75)
  Pallas kernels: 125 us -> 86.9 us
    pallas_call x1, Pallas kernels: 43 us -> 13.5 us  [finish(): pl.pallas_call(functools.partial(finish_kernel, order), grid=(length // t...]
    pallas_call x2, Pallas kernels: 39.2 us -> 29.5 us  [product(): pl.pallas_call(functools.partial(product_kernel, second, slots, per_step)...]
where the time goes in v3:
time: 114 us; the launch traced here: 113 us
  Pallas kernels  86.9 us (76%)
  starting transfers between devices  13.1 us (11%)
  waiting for transfers between devices  6.4 us (6%)
  local copies, waits for them, and re-layouts  4.08 us (4%)
  between operations  1.98 us (2%)
    pallas_call x1, Pallas kernels, gather_gram(): pl.pallas_call(gather_gram_kernel, out_shape=(jax.ShapeDtypeStruct((cols,...  43.9 us
    pallas_call x2, Pallas kernels, product(): pl.pallas_call(functools.partial(product_kernel, second, slots, per_step)...  29.5 us
    pallas_call x1, Pallas kernels, finish(): pl.pallas_call(functools.partial(finish_kernel, order), grid=(length // t...  13.5 us
    ppermute x2, starting transfers between devices, halo(): before = lax.ppermute(array[:, length - width:], 'row', up)  10.5 us
    ppermute x2, waiting for transfers between devices, halo(): before = lax.ppermute(array[:, length - width:], 'row', up)  4.67 us
    ppermute x2, starting transfers between devices, halo(): after = lax.ppermute(array[:, :width], 'row', down)  2.58 us
  transfers between devices with their start and end apart: 4, of which 3 were waited for; matrix products, arithmetic and copies ran while one was open for 1% of the time, Pallas kernels for 0%

profile of v3, /device:TPU:0, one launch (start us, length us, event | category | flops | bytes accessed | tf_op | source)
XLA Modules:
  0.0 113.1 jit_solution(16116288198273087032)
XLA Ops:
  0.6 1.0 fusion.1
  1.6 1.3 %collective-permute-start.1 = (bf16[64,1024]{1,0:T(8,128)(2,1)S(1)}, bf16[64,1024]{1,0:T(8,128)(2,1)S(1)}, u32[]{:S(2)}, u32[]{:S(2)}) collective-permute-start(bf16[64,1024]{1,0:T(8,128)(2,1)S(1)} %get-tuple-element.8), channel_id=1, source_target_pairs={{4,0},{8,4},{12,8},{16,12},{20,16},{24,20},{28,24},{5,1},{9,5},{13... | collective-permute-start | bytes 393224 | tf_op jit(solution)/shard_map/ppermute | solution.py:23
  2.9 5.5 %collective-permute-start = (bf16[64,1024]{1,0:T(8,128)(2,1)S(1)}, bf16[64,1024]{1,0:T(8,128)(2,1)S(1)}, u32[]{:S(2)}, u32[]{:S(2)}) collective-permute-start(bf16[64,1024]{1,0:T(8,128)(2,1)S(1)} %get-tuple-element.9), channel_id=1, source_target_pairs={{0,4},{4,8},{8,12},{12,16},{16,20},{20,24},{24,28},{1,5},{5,9},{9,... | collective-permute-start | bytes 393224 | tf_op jit(solution)/shard_map/ppermute | solution.py:22
  9.7 0.7 subtract_add_fusion
  10.4 0.1 copy.8
  10.5 0.7 reshape.14.index
  11.2 0.0 collective-permute-done.1.after
  11.2 0.0 copy-start
  11.2 1.7 %collective-permute-done.before = bf16[64,1024]{1,0:T(8,128)(2,1)S(1)} collective-permute-done((bf16[64,1024]{1,0:T(8,128)(2,1)S(1)}, bf16[64,1024]{1,0:T(8,128)(2,1)S(1)}, u32[]{:S(2)}, u32[]{:S(2)}) %collective-permute-start) | collective-permute-done | bytes 131104 | tf_op jit(solution)/shard_map/ppermute | solution.py:22
  12.9 0.0 copy-done
  12.9 0.0 copy-start.1
  12.9 0.7 copy-done.1
  13.6 14.7 %shard_map.77.field = bf16[64,8192]{1,0:T(8,128)(2,1)} custom-call(s32[768]{0:T(1024)} %reshape.14.index, s32[64]{0:T(128)} %live.3, f32[1]{0:T(128)S(6)} %copy.9.shift, f32[1]{0:T(128)S(6)} %copy.10.scale, bf16[64,12,128,128]{3,2,1,0:T(8,128)(2,1)} %blocks.3, bf16[64,1024]{1,0:T(8,128)(2,1)} %copy-done.1, bf16[64,8192]{1,0:T(8,128)(2,1)} %rest_0_.1, ...), custom_call_target="tpu_custom_call" | custom-call | flops 1610612736 | bytes 25165824 | tf_op jit(solution)/shard_map/pallas_call | solution.py:71
  28.3 1.0 fusion
  29.3 1.3 %collective-permute-start.3 = (bf16[64,1024]{1,0:T(8,128)(2,1)S(1)}, bf16[64,1024]{1,0:T(8,128)(2,1)S(1)}, u32[]{:S(2)}, u32[]{:S(2)}) collective-permute-start(bf16[64,1024]{1,0:T(8,128)(2,1)S(1)} %get-tuple-element.6), channel_id=1, source_target_pairs={{4,0},{8,4},{12,8},{16,12},{20,16},{24,20},{28,24},{5,1},{9,5},{13... | collective-permute-start | bytes 393224 | tf_op jit(solution)/shard_map/ppermute | solution.py:23
  30.6 5.0 %collective-permute-start.2 = (bf16[64,1024]{1,0:T(8,128)(2,1)S(1)}, bf16[64,1024]{1,0:T(8,128)(2,1)S(1)}, u32[]{:S(2)}, u32[]{:S(2)}) collective-permute-start(bf16[64,1024]{1,0:T(8,128)(2,1)S(1)} %get-tuple-element.7), channel_id=1, source_target_pairs={{0,4},{4,8},{8,12},{12,16},{16,20},{20,24},{24,28},{1,5},{5,9},{9,... | collective-permute-start | bytes 393224 | tf_op jit(solution)/shard_map/ppermute | solution.py:22
  35.6 1.7 %collective-permute-done.3.after = bf16[64,1024]{1,0:T(8,128)(2,1)S(1)} collective-permute-done((bf16[64,1024]{1,0:T(8,128)(2,1)S(1)}, bf16[64,1024]{1,0:T(8,128)(2,1)S(1)}, u32[]{:S(2)}, u32[]{:S(2)}) %collective-permute-start.3) | collective-permute-done | bytes 131104 | tf_op jit(solution)/shard_map/ppermute | solution.py:23
  37.4 0.0 copy-start.2
  37.4 3.0 %collective-permute-done.2.before = bf16[64,1024]{1,0:T(8,128)(2,1)S(1)} collective-permute-done((bf16[64,1024]{1,0:T(8,128)(2,1)S(1)}, bf16[64,1024]{1,0:T(8,128)(2,1)S(1)}, u32[]{:S(2)}, u32[]{:S(2)}) %collective-permute-start.2) | collective-permute-done | bytes 131104 | tf_op jit(solution)/shard_map/ppermute | solution.py:22
  40.3 0.0 copy-done.2
  40.3 0.7 copy-done.3
  41.0 14.8 %shard_map.78.own = bf16[64,8192]{1,0:T(8,128)(2,1)} custom-call(s32[768]{0:T(1024)} %reshape.14.index, s32[64]{0:T(128)} %live.3, f32[1]{0:T(128)S(6)} %copy.9.shift, f32[1]{0:T(128)S(6)} %copy.10.scale, bf16[64,12,128,128]{3,2,1,0:T(8,128)(2,1)} %blocks.3, bf16[64,1024]{1,0:T(8,128)(2,1)} %copy-done.3, bf16[64,8192]{1,0:T(8,128)(2,1)} %shard_map.77.field, ...), custom_call_target="tpu_custom_call" | custom-call | flops 1610612736 | bytes 25165824 | tf_op jit(solution)/shard_map/pallas_call | solution.py:71
  55.8 43.9 %shard_map.79 = (bf16[4,64,8192]{2,1,0:T(8,128)(2,1)}, f32[256,256]{1,0:T(8,128)}) custom-call(bf16[64,8192]{1,0:T(8,128)(2,1)} %shard_map.78.own), custom_call_target="tpu_custom_call" | custom-call | tf_op jit(solution)/shard_map/pallas_call | solution.py:349
  99.6 13.5 %shard_map.80 = (f32[64,8192]{1,0:T(8,128)}, f32[256,256]{1,0:T(8,128)}) custom-call(s32[1]{0:T(128)} %bitcast.own_group, f32[256,256]{1,0:T(8,128)} %get-tuple-element.4.gram, bf16[256,8192]{1,0:T(8,128)(2,1)} %bitcast.2), custom_call_target="tpu_custom_call" | custom-call | tf_op jit(solution)/shard_map/pallas_call | solution.py:182
  (1 shorter events, 0.0 us)
Async XLA Ops:
  1.6 9.6 %collective-permute-start.1 = (bf16[64,1024]{1,0:T(8,128)(2,1)S(1)}, bf16[64,1024]{1,0:T(8,128)(2,1)S(1)}, u32[]{:S(2)}, u32[]{:S(2)}) collective-permute-start(bf16[64,1024]{1,0:T(8,128)(2,1)S(1)} %get-tuple-element.8), channel_id=1, source_target_pairs={{4,0},{8,4},{12,8},{16,12},{20,16},{24,20},{28,24},{5,1},{9,5},{13... | collective-permute-start | bytes 393224 | tf_op jit(solution)/shard_map/ppermute | solution.py:23
  2.9 10.0 %collective-permute-start = (bf16[64,1024]{1,0:T(8,128)(2,1)S(1)}, bf16[64,1024]{1,0:T(8,128)(2,1)S(1)}, u32[]{:S(2)}, u32[]{:S(2)}) collective-permute-start(bf16[64,1024]{1,0:T(8,128)(2,1)S(1)} %get-tuple-element.9), channel_id=1, source_target_pairs={{0,4},{4,8},{8,12},{12,16},{16,20},{20,24},{24,28},{1,5},{5,9},{9,... | collective-permute-start | bytes 393224 | tf_op jit(solution)/shard_map/ppermute | solution.py:22
  11.2 1.7 %copy-start = (bf16[64,1024]{1,0:T(8,128)(2,1)}, bf16[64,1024]{1,0:T(8,128)(2,1)S(1)}, u32[]{:S(2)}) copy-start(bf16[64,1024]{1,0:T(8,128)(2,1)S(1)} %collective-permute-done.1.after) | copy-start | bytes 393220
  12.9 0.7 copy-start.1
  29.3 8.1 %collective-permute-start.3 = (bf16[64,1024]{1,0:T(8,128)(2,1)S(1)}, bf16[64,1024]{1,0:T(8,128)(2,1)S(1)}, u32[]{:S(2)}, u32[]{:S(2)}) collective-permute-start(bf16[64,1024]{1,0:T(8,128)(2,1)S(1)} %get-tuple-element.6), channel_id=1, source_target_pairs={{4,0},{8,4},{12,8},{16,12},{20,16},{24,20},{28,24},{5,1},{9,5},{13... | collective-permute-start | bytes 393224 | tf_op jit(solution)/shard_map/ppermute | solution.py:23
  30.6 9.7 %collective-permute-start.2 = (bf16[64,1024]{1,0:T(8,128)(2,1)S(1)}, bf16[64,1024]{1,0:T(8,128)(2,1)S(1)}, u32[]{:S(2)}, u32[]{:S(2)}) collective-permute-start(bf16[64,1024]{1,0:T(8,128)(2,1)S(1)} %get-tuple-element.7), channel_id=1, source_target_pairs={{0,4},{4,8},{8,12},{12,16},{16,20},{20,24},{24,28},{1,5},{5,9},{9,... | collective-permute-start | bytes 393224 | tf_op jit(solution)/shard_map/ppermute | solution.py:22
  37.4 3.0 %copy-start.2 = (bf16[64,1024]{1,0:T(8,128)(2,1)}, bf16[64,1024]{1,0:T(8,128)(2,1)S(1)}, u32[]{:S(2)}) copy-start(bf16[64,1024]{1,0:T(8,128)(2,1)S(1)} %collective-permute-done.3.after) | copy-start | bytes 393220
  40.3 0.7 copy-start.3
